TPU v7x, 512 devices: a whole 4x8x8 slice. The times are simulated.
512 devices in a mesh: dp: 128 (over z, y, core), proto: 4 (over x).
Axes of the slice: x: 4, y: 8, z: 8, core: 2. Of those that a mesh axis runs over, the one named last changes fastest.
Arguments:
- view_embed: bfloat16 [32768, 128], P('dp'), may hold values from -60 to 60
- pair_slot: int32 [16384, 2], P('dp'), may hold values from 0 to 255, as said below
- prototypes: bfloat16 [32768, 128], P('proto'), may hold values from -40 to 40
Outputs:
- possession_loss: float32 [16384], P('dp')
- proto_grad: bfloat16 [32768, 128], P('proto')
Inputs may be any that keep to these rules, and one draw needn't show every extreme that they name: `pair_slot`: within each aligned block of 128 possessions, the 256 entries name each of that block's view slots once.
All inputs are finite; a program needn't handle non-finite values.
Results may differ from a plain program's by a relative error of at most 0.0063.
Values may be sent and summed in bfloat16 or wider, within the bound.
A program may use at most 64 MiB of HBM per device.

v0:
```python
import jax
import jax.numpy as jnp
from jax import lax
from jax.sharding import PartitionSpec as P

SINK_ITERS = 3


sink_eps = 0.05
temper = 0.1
norm_eps = 1e-06


def unit_rows(matrix):
    widened = matrix.astype(jnp.float32)
    factor = lax.rsqrt(jnp.sum(widened * widened, axis=-1, keepdims=True) + norm_eps)
    return (widened * factor).astype(jnp.bfloat16)


def row_sum(partial_rows):
    return lax.psum(partial_rows, "proto")


def last_rows(partial_rows, partial_spread):
    return lax.psum((partial_rows, partial_spread), "proto")


def local(view_embed, pair_slot, prototypes):
    count_rows = pair_slot.shape[0]
    feature = view_embed.shape[1]
    local_k = prototypes.shape[0]
    block_k = min(local_k, 2048)
    blocks = local_k // block_k
    chosen = view_embed[pair_slot]
    unit_z = unit_rows(jnp.transpose(chosen, (1, 0, 2)).reshape(2 * count_rows, feature))
    proto_tiles = unit_rows(prototypes).reshape(blocks, block_k, feature)

    def scores_of(proto_tile):
        return lax.dot_general(
            unit_z, proto_tile, (((1,), (1,)), ((), ())), preferred_element_type=jnp.float32
        )

    def column_layout(col_scale):
        return jnp.transpose(col_scale.reshape(2, blocks, block_k), (1, 0, 2))

    row_scale = jnp.ones((2 * count_rows,), jnp.float32)
    col_scale = jnp.ones((2, local_k), jnp.float32)
    spread_total = row_scale
    for iteration in range(SINK_ITERS):
        is_last = iteration == SINK_ITERS - 1

        def column_block(proto_tile):
            weighted = row_scale[:, None] * jnp.exp(scores_of(proto_tile) / sink_eps)
            return jnp.sum(weighted.reshape(2, count_rows, block_k), axis=1)

        parts = lax.map(column_block, proto_tiles)
        col_scale = 1.0 / lax.psum(jnp.transpose(parts, (1, 0, 2)).reshape(2, local_k), "dp")

        def advance(running, element):
            proto_tile, scale_tile = element
            scores = scores_of(proto_tile)
            exponent = jnp.exp(scores / sink_eps).reshape(2, count_rows, block_k)
            row_part = running[0] + jnp.sum(exponent * scale_tile[:, None, :], axis=2).reshape(
                2 * count_rows
            )
            if is_last:
                spread = running[1] + jnp.sum(jnp.exp(scores / temper), axis=1)
            else:
                spread = running[1]
            return ((row_part, spread), None)

        totals, unused = lax.scan(
            advance,
            (jnp.zeros((2 * count_rows,), jnp.float32), jnp.zeros((2 * count_rows,), jnp.float32)),
            (proto_tiles, column_layout(col_scale)),
        )
        row_part, spread = totals
        if is_last:
            row_total, spread_total = last_rows(row_part, spread)
        else:
            row_total = row_sum(row_part)
        row_scale = 1.0 / row_total
    log_total = jnp.log(spread_total).reshape(2, count_rows)

    def final_step(running, element):
        proto_tile, scale_tile = element
        scores = scores_of(proto_tile).reshape(2, count_rows, block_k)
        exponent = jnp.exp(scores / sink_eps)
        assign = row_scale.reshape(2, count_rows)[:, :, None] * exponent * scale_tile[:, None, :]
        predict = jnp.exp(scores / temper - log_total[:, :, None])
        swapped = assign[::-1]
        coefficient = (
            ((predict - swapped) / temper).astype(jnp.bfloat16).reshape(2 * count_rows, block_k)
        )
        grad_tile = lax.dot_general(
            coefficient, unit_z, (((0,), (0,)), ((), ())), preferred_element_type=jnp.float32
        )
        cross_part = running[0] + jnp.sum(swapped * scores, axis=2)
        mass_part = running[1] + jnp.sum(swapped, axis=2)
        return ((cross_part, mass_part), grad_tile)

    initial = (jnp.zeros((2, count_rows), jnp.float32), jnp.zeros((2, count_rows), jnp.float32))
    (cross_part, mass_part), pieces = lax.scan(
        final_step, initial, (proto_tiles, column_layout(col_scale))
    )
    summed = lax.psum_scatter(
        pieces.reshape(local_k, feature), "dp", scatter_dimension=0, tiled=True
    )
    proto_grad = lax.all_gather(summed.astype(jnp.bfloat16), "dp", axis=0, tiled=True)
    cross_total, mass_total = lax.psum((cross_part, mass_part), "proto")
    possession_loss = -0.5 * jnp.sum(cross_total / temper - log_total * mass_total, axis=0)
    return (possession_loss, proto_grad)


def solution(mesh):
    placed = (P("dp", None), P("dp", None), P("proto", None))
    return jax.shard_map(
        local, mesh=mesh, in_specs=placed, out_specs=(P("dp"), P("proto", None)), check_vma=False
    )
```

profile of v0, /device:TPU:1, one launch (start us, length us, event | category | flops | bytes accessed | tf_op | source)
XLA Modules:
  0.0 968.7 jit_solution(4869716482841852236)
XLA Ops:
  9.4 2.9 fusion.38
  12.4 3.5 fusion.39
  18.8 186.2 %all-reduce.6.cloned.1.call-done = f32[2,8192]{1,0:T(2,128)} async-done(((f32[2,8192]{1,0:T(2,128)}), f32[2,8192]{1,0:T(2,128)}) %all-reduce.6.cloned.1.call-update) | async-done | bytes 65552 | tf_op jit(solution)/shard_map/psum | solution.py:57
  205.9 2.6 copy.20
  208.5 26.5 %while.83 = (s32[]{:T(128)}, f32[256]{0:T(256)S(1)}, bf16[4,2048,128]{2,1,0:T(8,128)(2,1)S(1)}, bf16[256,128]{1,0:T(8,128)(2,1)S(1)}, f32[4,2,2048]{1,2,0:T(8,128)}, /*index=5*/s32[]{:T(128)}, s32[]{:T(128)}) while((s32[]{:T(128)}, f32[256]{0:T(256)S(1)}, bf16[4,2048,128]{2,1,0:T(8,128)(2,1)S(1)}, bf16[256,128]{1,0:T(8,128)(2,1)S(1)}, ...), condition=%wide.region_8.9_spmd.clone, body=%wide.region_6.8_spmd.clone.sunk | while | flops 135790848 | bytes 4837471 | solution.py:72
  209.8 4.7 mul.211
  216.5 4.7 mul.211
  223.1 4.7 mul.211
  229.7 4.7 mul.211
  235.0 8.3 psum.64
  243.4 2.4 while.81
  246.5 173.4 %all-reduce.8.cloned.1.call-done = f32[2,8192]{1,0:T(2,128)} async-done(((f32[2,8192]{1,0:T(2,128)}), f32[2,8192]{1,0:T(2,128)}) %all-reduce.8.cloned.1.call-update) | async-done | bytes 65552 | tf_op jit(solution)/shard_map/psum | solution.py:57
  420.8 2.6 copy.21
  423.4 26.5 %while.84 = (s32[]{:T(128)}, f32[256]{0:T(256)S(1)}, bf16[4,2048,128]{2,1,0:T(8,128)(2,1)S(1)}, bf16[256,128]{1,0:T(8,128)(2,1)S(1)}, f32[4,2,2048]{1,2,0:T(8,128)}, /*index=5*/s32[]{:T(128)}, s32[]{:T(128)}) while((s32[]{:T(128)}, f32[256]{0:T(256)S(1)}, bf16[4,2048,128]{2,1,0:T(8,128)(2,1)S(1)}, ...), condition=%wide.region_16.17_spmd.clone, body=%wide.region_14.16_spmd.clone.sunk | while | flops 135790848 | bytes 4837471 | solution.py:72
  424.7 4.7 mul.213
  431.3 4.7 mul.213
  437.9 4.7 mul.213
  444.6 4.7 mul.213
  449.9 8.3 psum.66
  458.3 2.4 while.82
  461.4 173.3 %all-reduce.10.cloned.1.call-done = f32[2,8192]{1,0:T(2,128)} async-done(((f32[2,8192]{1,0:T(2,128)}), f32[2,8192]{1,0:T(2,128)}) %all-reduce.10.cloned.1.call-update) | async-done | bytes 65552 | tf_op jit(solution)/shard_map/psum | solution.py:57
  635.7 24.3 %while.85 = (s32[]{:T(128)}, f32[256]{0:T(256)S(1)}, f32[256]{0:T(256)S(1)}, bf16[4,2048,128]{2,1,0:T(8,128)(2,1)S(1)}, bf16[256,128]{1,0:T(8,128)(2,1)S(1)}, /*...) while((s32[]{:T(128)}, f32[256]{0:T(256)S(1)}, f32[256]{0:T(256)S(1)}, ...), condition=%wide.region_25.26_spmd.clone, body=%wide.region_22.25_spmd.clone.sunk | while | flops 136839680 | bytes 9068647 | solution.py:72
  636.1 4.7 mul.215
  642.2 4.7 mul.215
  648.2 4.7 mul.215
  654.3 4.7 mul.215
  660.0 8.3 all-reduce.1
  668.4 12.1 %while.86 = (s32[]{:T(128)}, f32[2,128]{1,0:T(2,128)S(1)}, f32[2,128]{1,0:T(2,128)S(1)}, f32[4,2048,128]{2,1,0:T(8,128)}, f32[256]{0:T(256)S(1)}, /*index=5*/bf1...) while((s32[]{:T(128)}, f32[2,128]{1,0:T(2,128)S(1)}, ...), condition=%wide.region_31.32_spmd.clone, body=%wide.region_28.31_spmd.clone.sunk | while | flops 274203136 | bytes 14379647 | solution.py:103
  680.5 189.4 %reduce-scatter.2.cloned.1.call-done = f32[64,128]{1,0:T(8,128)} async-done(((f32[8192,128]{1,0:T(8,128)}), f32[64,128]{1,0:T(8,128)}) %reduce-scatter.2.cloned.1.call-update) | async-done | bytes 32784 | tf_op jit(solution)/shard_map/reduce_scatter | solution.py:106
  871.3 8.4 all-reduce
  880.2 78.9 %all-gather.2.cloned.1.call-done = bf16[8192,128]{1,0:T(8,128)(2,1)} async-done(((bf16[64,128]{1,0:T(8,128)(2,1)}), bf16[8192,128]{1,0:T(8,128)(2,1)}) %all-gather.2.cloned.1.call-update) | async-done | bytes 2097168 | tf_op jit(solution)/shard_map/all_gather | solution.py:109
  959.1 3.0 copy.105
  (146 shorter events, 50.5 us)
Async XLA Ops:
  7.2 1.0 copy-start
  7.2 197.9 %all-reduce.6.cloned.1.call-start = ((), (), s32[]{:S(2)}) async-start(), calls=%async_computation.1 | async-start | bytes 131072 | tf_op jit(solution)/shard_map/psum | solution.py:57
  9.4 2.9 copy-start.1
  18.1 0.6 copy-start.3
  18.7 401.1 %all-reduce.8.cloned.1.call-start = ((), (), s32[]{:S(2)}) async-start(), calls=%async_computation.2 | async-start | bytes 131072 | tf_op jit(solution)/shard_map/psum | solution.py:57
  245.8 0.6 copy-start.4
  246.4 388.3 %all-reduce.10.cloned.1.call-start = ((), (), s32[]{:S(2)}) async-start(), calls=%async_computation.3 | async-start | bytes 131072 | tf_op jit(solution)/shard_map/psum | solution.py:57
  460.6 0.6 copy-start.2
  461.3 408.6 %reduce-scatter.2.cloned.1.call-start = ((), (), s32[]{:S(2)}) async-start(), calls=%async_computation.4 | async-start | bytes 4227072 | tf_op jit(solution)/shard_map/reduce_scatter | solution.py:106
  680.4 278.7 %all-gather.2.cloned.1.call-start = ((), (), s32[]{:S(2)}) async-start(), calls=%async_computation.5 | async-start | bytes 2113536 | tf_op jit(solution)/shard_map/all_gather | solution.py:109
Sparse Core Ops, SparseCore 0:
  18.9 186.1 all-reduce.5
  246.6 173.2 all-reduce.7
  461.4 173.2 all-reduce.9
  680.6 189.2 reduce-scatter.1
  873.9 85.1 all-gather.1
where the time goes:
time: 969 us
  waiting for transfers between devices  801 us (83%)
  local copies, waits for them, and re-layouts  79.7 us (8%)
  blocking collectives  33.4 us (3%)
  matrix products  21.7 us (2%)
  other arithmetic  17.4 us (2%)
  between operations  14 us (1%)
    psum x3, waiting for transfers between devices, local(): lax.psum(jnp.transpose(parts, (1, 0, 2)).reshape(2, local_k), 'dp')  533 us
    reduce_scatter x1, waiting for transfers between devices, local(): lax.psum_scatter(pieces.reshape(local_k, feature), 'dp', scatter_dimensio...  189 us
    all_gather x1, waiting for transfers between devices, local(): lax.all_gather(summed.astype(jnp.bfloat16), 'dp', axis=0, tiled=True)  78.9 us
    mul x20, local copies, waits for them, and re-layouts, advance(): exponent * scale_tile[:, None, :]  66.5 us
  transfers between devices with their start and end apart: 5, of which 5 were waited for; matrix products, arithmetic and copies ran while one was open for 0% of the time, Pallas kernels for 0%

commit v1 on v0

v1 whole, which is shorter than its diff:
```python
import jax
import jax.numpy as jnp
from jax import lax
from jax.experimental import pallas as pl
from jax.experimental.pallas import tpu as pltpu
from jax.sharding import PartitionSpec as P

MESH = pl.DeviceIdType.MESH
F32 = jnp.float32
BF16 = jnp.bfloat16
X, Y, Z = 4, 8, 8
L = 128
ITERS = 3
EPS = 1e-6


def coords():
    dp = lax.axis_index("dp")
    return lax.axis_index("proto"), (dp // 2) % Y, dp // (2 * Y), dp % 2


def device(x, y, z, c):
    return ((z * Y + y) * 2 + c, x)


def across(row):
    return jnp.transpose(jnp.broadcast_to(row, (L, L)))


def unit(wide):
    return (wide * lax.rsqrt(jnp.sum(wide * wide, axis=-1, keepdims=True) + EPS)).astype(BF16)


def kernel(
    view_ref, slot_ref, proto_ref, loss_ref, grad_ref,
    raw, unit_c, z_own, z_mine, z_other, expo, soft, weighted, z_scaled, grad_soft,
    col_part, col_send, col_got, col_scale, row_got, row_part, row_scale,
    half_send, half_got, half_own, half_out, piece_got, shard, whole, loss_rows, loss_send, loss_got,
    raw_sem, z_send, z_recv, o_send, o_recv, col_ssem, col_rsem, row_ssem, row_rsem,
    half_ssem, half_rsem, piece_ssem, piece_rsem, all_ssem, all_rsem, near_ssem, near_rsem,
    pass_ssem, pass_rsem, loss_ssem, loss_rsem, out_sem,
):
    x, y, z, c = coords()
    yb, zb, yh, zh = y % 2, z % 2, y // 2, z // 2
    quad = zb * 2 + yb
    row_me = (x * 2 + yb) * 2 + zb
    col_me = zh * (Y // 2) + yh
    n_row, n_col = X * 4, (Y // 2) * (Z // 2)
    sibling = device(x, y, z, 1 - c)

    def row_peer(step):
        t = (row_me + step) % n_row
        return device(t // 4, yh * 2 + (t // 2) % 2, zh * 2 + t % 2, c)

    def col_peer(step):
        t = (col_me + step) % n_col
        return t, device(x, (t % (Y // 2)) * 2 + yb, (t // (Y // 2)) * 2 + zb, c)

    def quad_peer(step, core):
        t = (quad + step) % 4
        return device(x, yh * 2 + t % 2, zh * 2 + t // 2, core)

    def near(dy, dz):
        return device(x, (y + dy) % Y, (z + dz) % Z, c)

    near_steps = [(1, 0), (-1, 0), (0, 1), (0, -1), (1, 1), (1, -1), (-1, 1), (-1, -1)]

    barrier = pltpu.get_barrier_semaphore()

    def hail(target):
        pl.semaphore_signal(barrier, inc=1, device_id=target, device_id_type=MESH)

    hail(sibling)
    for step in range(1, 4):
        hail(quad_peer(step, 0))
        hail(quad_peer(step, 1))
    for dy, dz in near_steps:
        hail(near(dy, dz))

    def hail_groups(step, unused):
        hail(row_peer(step))
        hail(col_peer(step)[1])
        return unused

    lax.fori_loop(1, 16, hail_groups, 0)

    fetch = pltpu.make_async_copy(proto_ref.at[pl.ds(quad * 2048, 2048)], raw, raw_sem)
    fetch.start()

    lanes = lax.broadcasted_iota(jnp.int32, (L, 2 * L), 1)
    for v in range(2):
        pick = (slot_ref[:, v : v + 1] == lanes).astype(F32).astype(BF16)
        z_own[v] = unit(jnp.dot(pick, view_ref[...], preferred_element_type=F32))
    pl.semaphore_wait(barrier, 45)

    place = quad * 2 + c
    z_mine[place] = z_own[c]
    pltpu.make_async_remote_copy(
        z_own.at[1 - c], z_mine.at[place], z_send, z_recv, device_id=sibling, device_id_type=MESH
    ).start()
    for step in range(1, 4):
        for core in range(2):
            pltpu.make_async_remote_copy(
                z_own.at[core], z_mine.at[place], z_send, z_recv,
                device_id=quad_peer(step, core), device_id_type=MESH,
            ).start()

    fetch.wait()

    def normalise(b, unused):
        unit_c[b] = unit(raw[pl.ds(b * L, L)].astype(F32))
        return unused

    lax.fori_loop(0, 16, normalise, 0)

    seven = z_mine.at[pl.ds(0, 7)]
    pltpu.make_async_copy(seven, seven, z_recv).wait()
    pltpu.make_async_copy(seven, seven, z_send).wait()
    to_other = pltpu.make_async_remote_copy(
        z_mine, z_other, o_send, o_recv, device_id=sibling, device_id_type=MESH
    )
    to_other.start()

    def dot_t(a, b):
        return lax.dot_general(a, b, (((1,), (1,)), ((), ())), preferred_element_type=F32)

    def fold(block):
        return jnp.sum(block.reshape(16, 8, block.shape[-1]), axis=0)

    def lay(part):
        row = jnp.sum(part, axis=0, keepdims=True)
        return jnp.concatenate([row[:, t * L : (t + 1) * L] for t in range(8)], axis=0)

    rows_z = z_mine[...].reshape(1024, L)

    def first(b, total):
        scores = dot_t(unit_c[b], rows_z)
        power = jnp.exp(scores * 10.0)
        soft[b] = power.astype(BF16)
        square = power * power
        expo[b] = square
        wide = square[:, 0:L]
        for t in range(1, 8):
            wide = wide + square[:, t * L : (t + 1) * L]
        col_part[pl.ds(b, 1)] = jnp.sum(jnp.transpose(wide), axis=0, keepdims=True)
        return total + fold(power)

    total_part = lax.fori_loop(0, 16, first, jnp.zeros((8, 1024), F32))

    def exchange_columns(it):
        col_send[it] = col_part[...].astype(BF16)
        got = col_got.at[it]
        got[col_me] = col_send[it]

        def send(step, unused):
            pltpu.make_async_remote_copy(
                col_send.at[it], got.at[col_me], col_ssem.at[it], col_rsem.at[it],
                device_id=col_peer(step)[1], device_id_type=MESH,
            ).start()
            return unused

        lax.fori_loop(1, n_col, send, 0)
        most = got.at[pl.ds(0, n_col - 1)]
        pltpu.make_async_copy(most, most, col_rsem.at[it]).wait()
        total = got[0].astype(F32)
        for m in range(1, n_col):
            total = total + got[m].astype(F32)
        col_scale[...] = 1.0 / total

    def exchange_rows(it, parts):
        row_part[it, 0:8] = parts[0]
        row_part[it, 8:16] = parts[1]
        got = row_got.at[it]
        got[row_me] = row_part[it]

        def send(step, unused):
            pltpu.make_async_remote_copy(
                row_part.at[it], got.at[row_me], row_ssem.at[it], row_rsem.at[it],
                device_id=row_peer(step), device_id_type=MESH,
            ).start()
            return unused

        lax.fori_loop(1, n_row, send, 0)
        most = got.at[pl.ds(0, n_row - 1)]
        pltpu.make_async_copy(most, most, row_rsem.at[it]).wait()
        total = got[0]
        for m in range(1, n_row):
            total = total + got[m]
        row_scale[...] = 1.0 / total[0:8]
        return total[0:8], total[8:16]

    def row_pass(b, acc):
        scale = across(col_scale[pl.ds(b, 1)])
        parts = [fold(expo[b, :, t * L : (t + 1) * L] * scale) for t in range(8)]
        return acc + jnp.concatenate(parts, axis=1)

    def col_pass(b, unused):
        wide = expo[b, :, 0:L] * row_scale[0:1]
        for t in range(1, 8):
            wide = wide + expo[b, :, t * L : (t + 1) * L] * row_scale[t : t + 1]
        col_part[pl.ds(b, 1)] = jnp.sum(jnp.transpose(wide), axis=0, keepdims=True)
        return unused

    zero = jnp.zeros((8, 1024), F32)

    exchange_columns(0)
    acc = lax.fori_loop(0, 16, row_pass, zero)
    total = exchange_rows(0, (lay(acc), lay(total_part)))[1]
    log_total = jnp.log(total)
    gain = 10.0 / total
    lax.fori_loop(0, 16, col_pass, 0)
    exchange_columns(1)
    acc = lax.fori_loop(0, 16, row_pass, zero)
    exchange_rows(1, (lay(acc), jnp.zeros((8, L), F32)))
    lax.fori_loop(0, 16, col_pass, 0)
    exchange_columns(2)

    for t in range(8):
        z_scaled[t] = (z_mine[t].astype(F32) * across(gain[t : t + 1])).astype(BF16)
    scaled = z_scaled[...].reshape(1024, L)

    def soft_grad(b, unused):
        grad_soft[b] = jnp.dot(soft[b], scaled, preferred_element_type=F32)
        return unused

    lax.fori_loop(0, 16, soft_grad, 0)
    to_other.wait()
    rows_o = z_other[...].reshape(1024, L)

    def last_pass(b, carry):
        acc, cross = carry
        scale = across(col_scale[pl.ds(b, 1)])
        other = dot_t(unit_c[b], rows_o)
        parts, crossed = [], []
        for t in range(8):
            here = expo[b, :, t * L : (t + 1) * L] * scale
            weighted[b, :, t * L : (t + 1) * L] = here.astype(BF16)
            parts.append(fold(here))
            crossed.append(fold(here * other[:, t * L : (t + 1) * L]))
        return acc + jnp.concatenate(parts, axis=1), cross + jnp.concatenate(crossed, axis=1)

    acc, cross = lax.fori_loop(0, 16, last_pass, (zero, zero))
    row_total, cross = exchange_rows(2, (lay(acc), lay(cross)))

    for t in range(8):
        z_scaled[t] = (z_other[t].astype(F32) * across(row_scale[t : t + 1] * 10.0)).astype(BF16)
    scaled = z_scaled[...].reshape(1024, L)

    def grad_block(b):
        return grad_soft[b] - jnp.dot(weighted[b], scaled, preferred_element_type=F32)

    def away(b, unused):
        half_send[b] = grad_block((1 - c) * 8 + b).astype(BF16)
        return unused

    lax.fori_loop(0, 8, away, 0)
    half = pltpu.make_async_remote_copy(
        half_send, half_got, half_ssem, half_rsem, device_id=sibling, device_id_type=MESH
    )
    half.start()

    def stay(b, unused):
        half_own[b] = grad_block(c * 8 + b)
        return unused

    lax.fori_loop(0, 8, stay, 0)

    scale = row_scale[...]
    loss_rows[0] = log_total
    loss_rows[1] = scale * cross
    loss_rows[2] = scale * row_total
    theirs = pl.ds(quad * 2 + (1 - c), 1)
    loss_send[...] = jnp.zeros((8, L), F32)
    for n in range(3):
        loss_send[n : n + 1] = loss_rows[n, theirs]
    loss_copy = pltpu.make_async_remote_copy(
        loss_send, loss_got, loss_ssem, loss_rsem, device_id=sibling, device_id_type=MESH
    )
    loss_copy.start()

    half.wait()
    half_out[...] = (half_own[...] + half_got[...].astype(F32)).astype(BF16).reshape(16, 64, L)

    def send_piece(step, unused):
        t, target = col_peer(step)
        pltpu.make_async_remote_copy(
            half_out.at[t], piece_got.at[col_me], piece_ssem, piece_rsem,
            device_id=target, device_id_type=MESH,
        ).start()
        return unused

    lax.fori_loop(1, n_col, send_piece, 0)
    piece_got[col_me] = half_out[col_me]

    loss_copy.wait()
    mine = pl.ds(place, 1)
    own_log, own_cross, own_mass = [loss_rows[n, mine] for n in range(3)]
    sib_log, sib_cross, sib_mass = [loss_got[n : n + 1] for n in range(3)]
    loss_ref[...] = -0.5 * (
        (own_cross + sib_cross) * 10.0 - own_log * sib_mass - sib_log * own_mass
    )

    most = piece_got.at[pl.ds(0, n_col - 1)]
    pltpu.make_async_copy(most, most, piece_rsem).wait()
    summed = piece_got[0].astype(F32)
    for m in range(1, n_col):
        summed = summed + piece_got[m].astype(F32)
    shard[...] = summed.astype(BF16)

    spot = whole.at[place]
    spot[pl.ds(col_me * 64, 64)] = shard[...]

    def send_shard(step, unused):
        pltpu.make_async_remote_copy(
            shard, spot.at[pl.ds(col_me * 64, 64)], all_ssem, all_rsem,
            device_id=col_peer(step)[1], device_id_type=MESH,
        ).start()
        return unused

    lax.fori_loop(1, n_col, send_shard, 0)
    bulk = spot.at[pl.ds(0, 960)]
    pltpu.make_async_copy(bulk, bulk, all_rsem).wait()

    kinds = [0, 0, 1, 1, 2, 2, 2, 2]
    starts = [0, 512, 0, 512, 0, 256, 512, 768]
    for (dy, dz), kind, start in zip(near_steps, kinds, starts):
        part = spot.at[pl.ds(start, 256 if kind == 2 else 512)]
        pltpu.make_async_remote_copy(
            part, part, near_ssem.at[kind], near_rsem.at[kind],
            device_id=near(dy, dz), device_id_type=MESH,
        ).start()

    def hand_over(which, sem):
        part = whole.at[which]
        pltpu.make_async_remote_copy(
            part, part, pass_ssem.at[sem], pass_rsem.at[sem], device_id=sibling, device_id_type=MESH
        ).start()

    def write_out(which, sem):
        pltpu.make_async_copy(
            whole.at[which], grad_ref.at[pl.ds(which * 1024, 1024)], out_sem.at[sem]
        ).start()

    hand_over(place, 0)
    write_out(place, 0)
    others = [zb * 2 + (1 - yb), (1 - zb) * 2 + yb, (1 - zb) * 2 + (1 - yb)]
    for kind, q in enumerate(others):
        got = whole.at[q * 2 + c]
        pltpu.make_async_copy(got, got, near_rsem.at[kind]).wait()
        hand_over(q * 2 + c, kind + 1)
        write_out(q * 2 + c, kind + 1)
    for n, q in enumerate([quad] + others):
        got = whole.at[q * 2 + (1 - c)]
        pltpu.make_async_copy(got, got, pass_rsem.at[n]).wait()
        write_out(q * 2 + (1 - c), n + 4)

    one = whole.at[0]
    for n in range(8):
        pltpu.make_async_copy(one, one, out_sem.at[n]).wait()
    for n in range(4):
        pltpu.make_async_copy(one, one, pass_ssem.at[n]).wait()
    for n in range(3):
        pltpu.make_async_copy(one, one, near_ssem.at[n]).wait()
    pltpu.make_async_copy(bulk, bulk, all_ssem).wait()
    pltpu.make_async_copy(most, most, piece_ssem).wait()
    for it in range(ITERS):
        part = col_got.at[it, pl.ds(0, n_col - 1)]
        pltpu.make_async_copy(part, part, col_ssem.at[it]).wait()
        part = row_got.at[it, pl.ds(0, n_row - 1)]
        pltpu.make_async_copy(part, part, row_ssem.at[it]).wait()


def local(view_embed, pair_slot, prototypes):
    vmem, dma = pltpu.VMEM, pltpu.SemaphoreType.DMA
    scratch = [
        vmem((2048, L), BF16),
        vmem((16, L, L), BF16),
        vmem((2, L, L), BF16),
        vmem((8, L, L), BF16),
        vmem((8, L, L), BF16),
        vmem((16, L, 1024), F32),
        vmem((16, L, 1024), BF16),
        vmem((16, L, 1024), BF16),
        vmem((8, L, L), BF16),
        vmem((16, L, L), F32),
        vmem((16, L), F32),
        vmem((ITERS, 16, L), BF16),
        vmem((ITERS, 16, 16, L), BF16),
        vmem((16, L), F32),
        vmem((ITERS, 16, 16, L), F32),
        vmem((ITERS, 16, L), F32),
        vmem((8, L), F32),
        vmem((8, L, L), BF16),
        vmem((8, L, L), BF16),
        vmem((8, L, L), F32),
        vmem((16, 64, L), BF16),
        vmem((16, 64, L), BF16),
        vmem((64, L), BF16),
        vmem((8, 1024, L), BF16),
        vmem((3, 8, L), F32),
        vmem((8, L), F32),
        vmem((8, L), F32),
        dma, dma, dma, dma, dma,
        dma((ITERS,)), dma((ITERS,)), dma((ITERS,)), dma((ITERS,)),
        dma, dma, dma, dma, dma, dma,
        dma((3,)), dma((3,)), dma((4,)), dma((4,)),
        dma, dma, dma((8,)),
    ]
    loss, grad = pl.pallas_call(
        kernel,
        out_shape=[
            jax.ShapeDtypeStruct((1, L), F32),
            jax.ShapeDtypeStruct((8192, L), BF16),
        ],
        in_specs=[
            pl.BlockSpec(memory_space=pltpu.VMEM),
            pl.BlockSpec(memory_space=pltpu.VMEM),
            pl.BlockSpec(memory_space=pl.ANY),
        ],
        out_specs=[
            pl.BlockSpec(memory_space=pltpu.VMEM),
            pl.BlockSpec(memory_space=pl.ANY),
        ],
        scratch_shapes=scratch,
        compiler_params=pltpu.CompilerParams(
            collective_id=0, has_side_effects=True, vmem_limit_bytes=48 << 20
        ),
        name="swav_step",
    )(view_embed, pair_slot, prototypes)
    return loss.reshape(L), grad


def solution(mesh):
    placed = (P("dp", None), P("dp", None), P("proto", None))
    return jax.shard_map(
        local, mesh=mesh, in_specs=placed, out_specs=(P("dp"), P("proto", None)), check_vma=False
    )
```

time: 969 us -> 118 us (0.12)
  waiting for transfers between devices: 801 us -> 0 us
  Pallas kernels: 0 us -> 112 us
  local copies, waits for them, and re-layouts: 79.7 us -> 5.04 us
  blocking collectives: 33.4 us -> 0 us
  matrix products: 21.7 us -> 0 us
  other arithmetic: 17.4 us -> 0 us
  between operations: 14 us -> 0.64 us
    psum x3 -> x0, waiting for transfers between devices: 533 us -> none  [local(): lax.psum(jnp.transpose(parts, (1, 0, 2)).reshape(2, local_k), 'dp')]
    reduce_scatter x1 -> x0, waiting for transfers between devices: 189 us -> none  [local(): lax.psum_scatter(pieces.reshape(local_k, feature), 'dp', scatter_dimensio...]
    pallas_call x0 -> x1, Pallas kernels: none -> 112 us  [local(): pl.pallas_call(kernel, out_shape=[jax.ShapeDtypeStruct((1, L), F32), jax....]
    all_gather x1 -> x0, waiting for transfers between devices: 78.9 us -> none  [local(): lax.all_gather(summed.astype(jnp.bfloat16), 'dp', axis=0, tiled=True)]
    mul x20 -> x0, local copies, waits for them, and re-layouts: 66.5 us -> none  [advance(): exponent * scale_tile[:, None, :]]
    psum x4 -> x0, blocking collectives: 33.4 us -> none  [the longest x2 16.7 us: row_sum(): return lax.psum(partial_rows, 'proto')]
    dot_general x32 -> x0, matrix products: 21.7 us -> none  [the longest x28 15.8 us: scores_of(): lax.dot_general(unit_z, proto_tile, (((1,), (1,)), ((), ())), preferred_e...]
  transfers between devices with their start and end apart: 5 -> 0, of which waited for: 5 -> 0; matrix products, arithmetic and copies ran while one was open for 0% -> 0% of each run, Pallas kernels for 0% -> 0%
where the time goes in v1:
time: 118 us
  Pallas kernels  112 us (95%)
  local copies, waits for them, and re-layouts  5.04 us (4%)
    pallas_call x1, Pallas kernels, local(): pl.pallas_call(kernel, out_shape=[jax.ShapeDtypeStruct((1, L), F32), jax....  112 us
    unnamed x7, local copies, waits for them, and re-layouts  5.04 us

profile of v1, /device:TPU:1, one launch (start us, length us, event | category | flops | bytes accessed | tf_op | source)
XLA Modules:
  0.0 117.6 jit_solution(975734053593527134)
XLA Ops:
  0.6 0.8 copy.5.slot_ref
  1.4 0.0 copy-start
  1.4 1.6 %copy-done = bf16[8192,128]{1,0:T(8,128)(2,1)S(1)} copy-done((bf16[8192,128]{1,0:T(8,128)(2,1)S(1)}, bf16[8192,128]{1,0:T(8,128)(2,1)}, u32[]{:S(2)}) %copy-start) | copy-done | bytes 2097176
  3.0 0.0 copy-start.1
  3.0 0.8 copy-done.1
  3.8 111.9 %swav_step.1 = (f32[1,128]{1,0:T(1,128)S(1)}, bf16[8192,128]{1,0:T(8,128)(2,1)S(1)}) custom-call(bf16[256,128]{1,0:T(8,128)(2,1)S(1)} %copy-done.1, s32[128,2]{1,0:T(8,128)S(1)} %copy.5.slot_ref, bf16[8192,128]{1,0:T(8,128)(2,1)S(1)} %copy-done), custom_call_target="tpu_custom_call" | custom-call | tf_op jit(solution)/shard_map/swav_step/pallas_call | solution.py:409
  115.8 0.5 copy.8
  116.3 1.3 %copy.9 = bf16[8192,128]{1,0:T(8,128)(2,1)} copy(bf16[8192,128]{1,0:T(8,128)(2,1)S(1)} %get-tuple-element.9) | data formatting | bytes 4194304
Async XLA Ops:
  1.4 1.6 %copy-start = (bf16[8192,128]{1,0:T(8,128)(2,1)S(1)}, bf16[8192,128]{1,0:T(8,128)(2,1)}, u32[]{:S(2)}) copy-start(bf16[8192,128]{1,0:T(8,128)(2,1)} %proto_ref.1) | copy-start | bytes 6291460
  3.0 0.8 copy-start.1

commit v2 on v0

v2 whole, which is shorter than its diff:
```python
import math

import jax
import jax.numpy as jnp
from jax import lax
from jax.experimental import pallas as pl
from jax.experimental.pallas import tpu as pltpu
from jax.sharding import PartitionSpec as P

MESH = pl.DeviceIdType.MESH
F32 = jnp.float32
BF16 = jnp.bfloat16
X, Y, Z = 4, 8, 8
L = 128
ITERS = 3
EPS = 1e-6
CHUNKS = 4
ROWS = 1024 // CHUNKS
PIECE = ROWS // 16


def coords():
    dp = lax.axis_index("dp")
    return lax.axis_index("proto"), (dp // 2) % Y, dp // (2 * Y), dp % 2


def device(x, y, z, c):
    return ((z * Y + y) * 2 + c, x)


def across(row):
    return jnp.transpose(jnp.broadcast_to(row, (L, L)))


def down(block):
    return jnp.sum(jnp.transpose(block), axis=0, keepdims=True)


def fold(block):
    return jnp.sum(block.reshape(-1, 8, block.shape[-1]), axis=0)


def unit(wide):
    return (wide * lax.rsqrt(jnp.sum(wide * wide, axis=-1, keepdims=True) + EPS)).astype(BF16)


def dot_t(a, b):
    return lax.dot_general(a, b, (((1,), (1,)), ((), ())), preferred_element_type=F32)


def copy_to(src, dst, send_sem, recv_sem, target):
    return pltpu.make_async_remote_copy(
        src, dst, send_sem, recv_sem, device_id=target, device_id_type=MESH
    )


def bytes_of(ref, sem):
    pltpu.make_async_copy(ref, ref, sem).wait()


def kernel(
    view_ref, slot_ref, proto_ref, loss_ref, grad_ref,
    view, slot, raw, unit_c, z_own, z_mine, z_other, expo, soft, weighted, z_scaled, grad_soft,
    col_wide, col_part, col_got, col_scale, row_part, row_got, row_scale, row_sum, more_part, more_got,
    half_send, half_got, half_own, half_out, piece_got, shard, whole, loss_rows, loss_send, loss_got,
    in_sem, z_send, z_recv, o_send, o_recv, col_ssem, col_rsem, row_ssem, row_rsem,
    more_ssem, more_rsem, half_ssem, half_rsem, piece_ssem, piece_rsem, all_ssem, all_rsem,
    near_ssem, near_rsem, pass_ssem, pass_rsem, loss_ssem, loss_rsem, out_sem,
):
    x, y, z, c = coords()
    yb, zb, yh, zh = y % 2, z % 2, y // 2, z // 2
    quad = zb * 2 + yb
    row_me = (x * 2 + yb) * 2 + zb
    col_me = zh * (Y // 2) + yh
    n_row, n_col = X * 4, (Y // 2) * (Z // 2)
    sibling = device(x, y, z, 1 - c)

    def row_peer(step):
        t = (row_me + step) % n_row
        return device(t // 4, yh * 2 + (t // 2) % 2, zh * 2 + t % 2, c)

    def col_peer(step):
        t = (col_me + step) % n_col
        return t, device(x, (t % (Y // 2)) * 2 + yb, (t // (Y // 2)) * 2 + zb, c)

    def block_chip(kind):
        return (yb + kind % 2) % 2, (zb + kind // 2) % 2

    def block_peer(kind, core):
        py, pz = block_chip(kind)
        return device(x, yh * 2 + py, zh * 2 + pz, core)

    def block_quad(kind):
        py, pz = block_chip(kind)
        return pz * 2 + py

    def near(dy, dz):
        return device(x, (y + dy) % Y, (z + dz) % Z, c)

    near_steps = [(1, 0), (-1, 0), (0, 1), (0, -1), (1, 1), (1, -1), (-1, 1), (-1, -1)]

    barrier = pltpu.get_barrier_semaphore()

    def hail(target):
        pl.semaphore_signal(barrier, inc=1, device_id=target, device_id_type=MESH)

    fetches = [
        pltpu.make_async_copy(slot_ref, slot, in_sem.at[0]),
        pltpu.make_async_copy(view_ref, view, in_sem.at[1]),
        pltpu.make_async_copy(proto_ref.at[pl.ds(quad * 2048, 2048)], raw, in_sem.at[2]),
    ]
    for fetch in fetches:
        fetch.start()

    def hail_groups(step, unused):
        hail(col_peer(step)[1])
        hail(row_peer(step))
        return unused

    lax.fori_loop(1, 16, hail_groups, 0)
    for dy, dz in near_steps:
        hail(near(dy, dz))
    for kind in range(1, 4):
        hail(block_peer(kind, 0))
        hail(block_peer(kind, 1))
    hail(sibling)

    fetches[0].wait()
    fetches[1].wait()
    lanes = lax.broadcasted_iota(jnp.int32, (L, 2 * L), 1).astype(F32)
    slots = slot[...].astype(F32)
    for v in range(2):
        chosen = across(slots[v : v + 1])
        pick = (jnp.concatenate([chosen, chosen], axis=1) == lanes).astype(F32).astype(BF16)
        z_own[v] = unit(jnp.dot(pick, view[...], preferred_element_type=F32))
    pl.semaphore_wait(barrier, 45)

    place = quad * 2 + c
    copy_to(z_own.at[1 - c], z_mine.at[place], z_send.at[0], z_recv.at[0], sibling).start()
    for kind in range(1, 4):
        for core in range(2):
            copy_to(
                z_own.at[core], z_mine.at[place], z_send.at[kind], z_recv.at[kind],
                block_peer(kind, core),
            ).start()
    z_mine[place] = z_own[c]
    fetches[2].wait()

    def normalise(b, unused):
        rows = pl.ds(b * 256, 256)
        unit_c[rows] = unit(raw[rows].astype(F32))
        return unused

    lax.fori_loop(0, 8, normalise, 0)

    def send_columns(it, h):
        def send(step, unused):
            copy_to(
                col_part.at[it, h], col_got.at[it, h, col_me], col_ssem.at[it, h],
                col_rsem.at[it, h], col_peer(step)[1],
            ).start()
            return unused

        lax.fori_loop(1, n_col, send, 0)
        col_got[it, h, col_me] = col_part[it, h]

    def wait_columns(it, h):
        bytes_of(col_got.at[it, h, pl.ds(0, n_col - 1)], col_rsem.at[it, h])
        total = col_got[it, h, 0]
        for m in range(1, n_col):
            total = total + col_got[it, h, m]
        col_scale[h] = 1.0 / total

    def first_block(q, rows_z, b):
        rows = pl.ds(b * 256, 256)
        scores = dot_t(unit_c[rows], rows_z)
        power = jnp.exp2(scores * (10.0 / math.log(2.0)))
        square = power * power
        soft[q, rows] = power.astype(BF16)
        expo[q, rows] = square
        return rows, square[:, :L] + square[:, L:], fold(power)

    for kind in range(4):
        q = block_quad(kind)
        got = z_mine.at[pl.ds(q * 2, 2)]
        bytes_of(z_mine.at[0] if kind == 0 else got, z_recv.at[kind])
        rows_z = z_mine[pl.ds(q * 2, 2)].reshape(256, L)

        def first(b, total, q=q, rows_z=rows_z, kind=kind):
            rows, wide, terms = first_block(q, rows_z, b)
            if kind == 0:
                col_wide[rows] = wide
            else:
                col_wide[rows] += wide
            return total + terms

        def first_last(b, total, q=q, rows_z=rows_z, h=0):
            rows, wide, terms = first_block(q, rows_z, h * 4 + b)
            wide = wide + col_wide[rows]
            col_part[0, h, pl.ds(b * 2, 1)] = down(wide[:L])
            col_part[0, h, pl.ds(b * 2 + 1, 1)] = down(wide[L:])
            return total + terms

        total = jnp.zeros((8, 256), F32)
        if kind < 3:
            total = lax.fori_loop(0, 8, first, total, unroll=2)
        else:
            for h in range(2):
                total = lax.fori_loop(
                    0, 4, lambda b, t, h=h: first_last(b, t, h=h), total, unroll=2
                )
                send_columns(0, h)
        terms = jnp.sum(total, axis=0, keepdims=True)
        more_part[0, pl.ds(q * 2, 1)] = terms[:, :L]
        more_part[0, pl.ds(q * 2 + 1, 1)] = terms[:, L:]

    for kind in range(4):
        bytes_of(z_mine.at[pl.ds(0, 1 if kind == 0 else 2)], z_send.at[kind])
    to_other = copy_to(z_mine, z_other, o_send, o_recv, sibling)
    to_other.start()

    def send_rows(part, got, ssem, rsem):
        def send(step, unused):
            copy_to(part, got.at[row_me], ssem, rsem, row_peer(step)).start()
            return unused

        lax.fori_loop(1, n_row, send, 0)
        got[row_me] = part[...]

    def wait_rows(got, rsem):
        bytes_of(got.at[pl.ds(0, n_row - 1)], rsem)
        total = got[0]
        for m in range(1, n_row):
            total = total + got[m]
        return total

    def row_pass(it, keep):
        acc = [jnp.zeros((8, 256), F32)] * 4
        for h in range(2):
            wait_columns(it, h)

            def step(b, acc, h=h):
                rows = pl.ds(h * 1024 + b * L, L)
                scale = across(col_scale[h, pl.ds(b, 1)])
                scale = jnp.concatenate([scale, scale], axis=1)
                new = []
                for q in range(4):
                    here = expo[q, rows] * scale
                    if keep:
                        weighted[q, rows] = here.astype(BF16)
                    new.append(acc[q] + fold(here))
                return new

            acc = lax.fori_loop(0, 8, step, acc, unroll=4)
        for q in range(4):
            sums = jnp.sum(acc[q], axis=0, keepdims=True)
            row_part[it, q * 2 : q * 2 + 1] = sums[:, :L]
            row_part[it, q * 2 + 1 : q * 2 + 2] = sums[:, L:]
        send_rows(row_part.at[it], row_got.at[it], row_ssem.at[it], row_rsem.at[it])

    def col_pass(it):
        for h in range(2):

            def step(b, unused, h=h):
                rows = pl.ds(h * 1024 + b * L, L)
                wide = None
                for q in range(4):
                    for s in range(2):
                        term = expo[q, rows, s * L : (s + 1) * L] * row_scale[2 * q + s : 2 * q + s + 1]
                        wide = term if wide is None else wide + term
                col_part[it, h, pl.ds(b, 1)] = down(wide)
                return unused

            lax.fori_loop(0, 8, step, 0, unroll=4)
            send_columns(it, h)

    row_pass(0, False)
    send_rows(more_part.at[0], more_got.at[0], more_ssem.at[0], more_rsem.at[0])
    row_scale[...] = 1.0 / wait_rows(row_got.at[0], row_rsem.at[0])
    col_pass(1)

    spread = wait_rows(more_got.at[0], more_rsem.at[0])
    loss_rows[0] = jnp.log(spread)
    gain = 10.0 / spread
    for t in range(8):
        z_scaled[t] = (z_mine[t].astype(F32) * across(gain[t : t + 1])).astype(BF16)

    def blocks_dot(left, rows):
        out = None
        for q in range(4):
            part = jnp.dot(
                left[q, rows], z_scaled[2 * q : 2 * q + 2].reshape(256, L), preferred_element_type=F32
            )
            out = part if out is None else out + part
        return out

    def soft_grad(b, unused):
        rows = pl.ds(b * 256, 256)
        grad_soft[rows] = blocks_dot(soft, rows)
        return unused

    lax.fori_loop(0, 8, soft_grad, 0)

    row_pass(1, False)
    row_scale[...] = 1.0 / wait_rows(row_got.at[1], row_rsem.at[1])
    col_pass(2)
    to_other.wait()
    row_pass(2, True)

    rows_o = [z_other[2 * q : 2 * q + 2].reshape(256, L) for q in range(4)]

    def cross_step(b, acc):
        rows = pl.ds(b * L, L)
        return [
            acc[q] + fold(weighted[q, rows].astype(F32) * dot_t(unit_c[rows], rows_o[q]))
            for q in range(4)
        ]

    acc = lax.fori_loop(0, 16, cross_step, [jnp.zeros((8, 256), F32)] * 4, unroll=2)
    for q in range(4):
        sums = jnp.sum(acc[q], axis=0, keepdims=True)
        more_part[1, q * 2 : q * 2 + 1] = sums[:, :L]
        more_part[1, q * 2 + 1 : q * 2 + 2] = sums[:, L:]
    row_total = wait_rows(row_got.at[2], row_rsem.at[2])
    scale = 1.0 / row_total
    row_scale[...] = scale
    row_sum[...] = row_total

    gain = scale * 10.0
    for t in range(8):
        z_scaled[t] = (z_other[t].astype(F32) * across(gain[t : t + 1])).astype(BF16)

    def grad_block(start):
        rows = pl.ds(start, ROWS)
        return grad_soft[rows] - blocks_dot(weighted, rows)

    def half_copy(m):
        return copy_to(half_send.at[m], half_got.at[m], half_ssem.at[m], half_rsem.at[m], sibling)

    def away(m):
        half_send[m] = grad_block((1 - c) * 1024 + m * ROWS).astype(BF16)
        half_copy(m).start()

    def stay(m):
        half_own[m] = grad_block(c * 1024 + m * ROWS)

    def scatter(m):
        half_copy(m).wait()
        both = half_own[m] + half_got[m].astype(F32)
        half_out[m] = both.astype(BF16).reshape(16, PIECE, L)

        def send(step, unused):
            t, target = col_peer(step)
            copy_to(
                half_out.at[m, t], piece_got.at[m, col_me], piece_ssem.at[m], piece_rsem.at[m], target
            ).start()
            return unused

        lax.fori_loop(1, n_col, send, 0)
        piece_got[m, col_me] = half_out[m, col_me]

    away(0)
    for m in range(CHUNKS):
        if m + 1 < CHUNKS:
            away(m + 1)
        stay(m)
        scatter(m)

    send_rows(more_part.at[1], more_got.at[1], more_ssem.at[1], more_rsem.at[1])
    cross = wait_rows(more_got.at[1], more_rsem.at[1])
    loss_rows[1] = row_scale[...] * cross
    loss_rows[2] = row_scale[...] * row_sum[...]
    theirs = pl.ds(quad * 2 + (1 - c), 1)
    loss_send[...] = jnp.zeros((8, L), F32)
    for n in range(3):
        loss_send[n : n + 1] = loss_rows[n, theirs]
    loss_copy = copy_to(loss_send, loss_got, loss_ssem, loss_rsem, sibling)
    loss_copy.start()

    def at_place(spot, m, start, count):
        return whole.at[spot, pl.ds(m * ROWS + start, count)]

    for m in range(CHUNKS):
        bytes_of(piece_got.at[m, pl.ds(0, n_col - 1)], piece_rsem.at[m])
        summed = piece_got[m, 0].astype(F32)
        for n in range(1, n_col):
            summed = summed + piece_got[m, n].astype(F32)
        shard[m] = summed.astype(BF16)

        def send_shard(step, unused, m=m):
            copy_to(
                shard.at[m], at_place(place, m, col_me * PIECE, PIECE), all_ssem.at[m],
                all_rsem.at[m], col_peer(step)[1],
            ).start()
            return unused

        lax.fori_loop(1, n_col, send_shard, 0)
        whole[place, pl.ds(m * ROWS + col_me * PIECE, PIECE)] = shard[m]

    loss_copy.wait()
    mine = pl.ds(place, 1)
    own_log, own_cross, own_mass = [loss_rows[n, mine] for n in range(3)]
    sib_log, sib_cross, sib_mass = [loss_got[n : n + 1] for n in range(3)]
    loss_ref[...] = -0.5 * (
        (own_cross + sib_cross) * 10.0 - own_log * sib_mass - sib_log * own_mass
    )

    kinds = [1, 1, 2, 2, 3, 3, 3, 3]
    half, fourth = ROWS // 2, ROWS // 4
    starts = [0, half, 0, half, 0, fourth, 2 * fourth, 3 * fourth]

    def hand_over(spot, m, kind):
        part = at_place(spot, m, 0, ROWS)
        copy_to(part, part, pass_ssem.at[kind, m], pass_rsem.at[kind, m], sibling).start()

    def write_out(spot, m):
        pltpu.make_async_copy(
            at_place(spot, m, 0, ROWS),
            grad_ref.at[pl.ds(spot * 1024 + m * ROWS, ROWS)],
            out_sem.at[spot, m],
        ).start()

    for m in range(CHUNKS):
        bytes_of(at_place(place, m, 0, ROWS - PIECE), all_rsem.at[m])
        for (dy, dz), kind, start in zip(near_steps, kinds, starts):
            part = at_place(place, m, start, fourth if kind == 3 else half)
            copy_to(
                part, part, near_ssem.at[kind - 1, m], near_rsem.at[kind - 1, m], near(dy, dz)
            ).start()
        hand_over(place, m, 0)
        write_out(place, m)
    for m in range(CHUNKS):
        for kind in range(1, 4):
            spot = block_quad(kind) * 2 + c
            bytes_of(at_place(spot, m, 0, ROWS), near_rsem.at[kind - 1, m])
            hand_over(spot, m, kind)
            write_out(spot, m)
    for m in range(CHUNKS):
        for kind in range(4):
            spot = block_quad(kind) * 2 + (1 - c)
            bytes_of(at_place(spot, m, 0, ROWS), pass_rsem.at[kind, m])
            write_out(spot, m)

    for m in range(CHUNKS):
        one = at_place(0, 0, 0, ROWS)
        for n in range(8):
            bytes_of(one, out_sem.at[n, m])
        for kind in range(4):
            bytes_of(one, pass_ssem.at[kind, m])
        for kind in range(3):
            bytes_of(one, near_ssem.at[kind, m])
        bytes_of(at_place(0, 0, 0, ROWS - PIECE), all_ssem.at[m])
        bytes_of(piece_got.at[m, pl.ds(0, n_col - 1)], piece_ssem.at[m])
    for it in range(ITERS):
        for h in range(2):
            bytes_of(col_got.at[it, h, pl.ds(0, n_col - 1)], col_ssem.at[it, h])
        bytes_of(row_got.at[it, pl.ds(0, n_row - 1)], row_ssem.at[it])
    for n in range(2):
        bytes_of(more_got.at[n, pl.ds(0, n_row - 1)], more_ssem.at[n])


def local(view_embed, pair_slot, prototypes):
    vmem, dma = pltpu.VMEM, pltpu.SemaphoreType.DMA
    scratch = [
        vmem((256, L), BF16),
        vmem((2, L), jnp.int32),
        vmem((2048, L), BF16),
        vmem((2048, L), BF16),
        vmem((2, L, L), BF16),
        vmem((8, L, L), BF16),
        vmem((8, L, L), BF16),
        vmem((4, 2048, 256), F32),
        vmem((4, 2048, 256), BF16),
        vmem((4, 2048, 256), BF16),
        vmem((8, L, L), BF16),
        vmem((2048, L), F32),
        vmem((2048, L), F32),
        vmem((ITERS, 2, 8, L), F32),
        vmem((ITERS, 2, 16, 8, L), F32),
        vmem((2, 8, L), F32),
        vmem((ITERS, 8, L), F32),
        vmem((ITERS, 16, 8, L), F32),
        vmem((8, L), F32),
        vmem((8, L), F32),
        vmem((2, 8, L), F32),
        vmem((2, 16, 8, L), F32),
        vmem((CHUNKS, ROWS, L), BF16),
        vmem((CHUNKS, ROWS, L), BF16),
        vmem((CHUNKS, ROWS, L), F32),
        vmem((CHUNKS, 16, PIECE, L), BF16),
        vmem((CHUNKS, 16, PIECE, L), BF16),
        vmem((CHUNKS, PIECE, L), BF16),
        vmem((8, 1024, L), BF16),
        vmem((3, 8, L), F32),
        vmem((8, L), F32),
        vmem((8, L), F32),
        dma((3,)), dma((4,)), dma((4,)), dma, dma,
        dma((ITERS, 2)), dma((ITERS, 2)), dma((ITERS,)), dma((ITERS,)),
        dma((2,)), dma((2,)),
        dma((CHUNKS,)), dma((CHUNKS,)), dma((CHUNKS,)), dma((CHUNKS,)),
        dma((CHUNKS,)), dma((CHUNKS,)),
        dma((3, CHUNKS)), dma((3, CHUNKS)), dma((4, CHUNKS)), dma((4, CHUNKS)),
        dma, dma, dma((8, CHUNKS)),
    ]
    loss, grad = pl.pallas_call(
        kernel,
        out_shape=[
            jax.ShapeDtypeStruct((1, L), F32),
            jax.ShapeDtypeStruct((8192, L), BF16),
        ],
        in_specs=[pl.BlockSpec(memory_space=pltpu.HBM)] * 3,
        out_specs=[
            pl.BlockSpec(memory_space=pltpu.VMEM),
            pl.BlockSpec(memory_space=pl.ANY),
        ],
        scratch_shapes=scratch,
        compiler_params=pltpu.CompilerParams(
            collective_id=0, has_side_effects=True, vmem_limit_bytes=50 << 20
        ),
        name="swav_step",
    )(view_embed, pair_slot.T, prototypes)
    return loss.reshape(L), grad


def solution(mesh):
    placed = (P("dp", None), P("dp", None), P("proto", None))
    return jax.shard_map(
        local, mesh=mesh, in_specs=placed, out_specs=(P("dp"), P("proto", None)), check_vma=False
    )
```

time: 969 us -> 98.6 us (0.10)
  waiting for transfers between devices: 801 us -> 0 us
  Pallas kernels: 0 us -> 94.5 us
  local copies, waits for them, and re-layouts: 79.7 us -> 3.34 us
  blocking collectives: 33.4 us -> 0 us
  matrix products: 21.7 us -> 0 us
  other arithmetic: 17.4 us -> 0 us
  between operations: 14 us -> 0.65 us
    psum x3 -> x0, waiting for transfers between devices: 533 us -> none  [local(): lax.psum(jnp.transpose(parts, (1, 0, 2)).reshape(2, local_k), 'dp')]
    reduce_scatter x1 -> x0, waiting for transfers between devices: 189 us -> none  [local(): lax.psum_scatter(pieces.reshape(local_k, feature), 'dp', scatter_dimensio...]
    pallas_call x0 -> x1, Pallas kernels: none -> 94.5 us  [local(): pl.pallas_call(kernel, out_shape=[jax.ShapeDtypeStruct((1, L), F32), jax....]
    all_gather x1 -> x0, waiting for transfers between devices: 78.9 us -> none  [local(): lax.all_gather(summed.astype(jnp.bfloat16), 'dp', axis=0, tiled=True)]
    mul x20 -> x0, local copies, waits for them, and re-layouts: 66.5 us -> none  [advance(): exponent * scale_tile[:, None, :]]
    psum x4 -> x0, blocking collectives: 33.4 us -> none  [the longest x2 16.7 us: row_sum(): return lax.psum(partial_rows, 'proto')]
    dot_general x32 -> x0, matrix products: 21.7 us -> none  [the longest x28 15.8 us: scores_of(): lax.dot_general(unit_z, proto_tile, (((1,), (1,)), ((), ())), preferred_e...]
  transfers between devices with their start and end apart: 5 -> 0, of which waited for: 5 -> 0; matrix products, arithmetic and copies ran while one was open for 0% -> 0% of each run, Pallas kernels for 0% -> 0%
where the time goes in v2:
time: 98.6 us; the launch traced here: 98.5 us
  Pallas kernels  94.5 us (96%)
  local copies, waits for them, and re-layouts  3.34 us (3%)
    pallas_call x1, Pallas kernels, local(): pl.pallas_call(kernel, out_shape=[jax.ShapeDtypeStruct((1, L), F32), jax....  94.5 us
    unnamed x6, local copies, waits for them, and re-layouts  3.34 us

profile of v2, /device:TPU:1, one launch (start us, length us, event | category | flops | bytes accessed | tf_op | source)
XLA Modules:
  0.0 98.5 jit_solution(5744959227619167006)
XLA Ops:
  0.6 0.0 copy-start
  0.6 0.8 copy-done
  1.5 0.0 copy-start.1
  1.5 0.7 copy-done.1
  2.1 94.5 %swav_step.1 = (f32[1,128]{1,0:T(1,128)S(1)}, bf16[8192,128]{1,0:T(8,128)(2,1)S(1)}) custom-call(bf16[256,128]{1,0:T(8,128)(2,1)S(1)} %copy-done, s32[2,128]{1,0:T(2,128)S(1)} %bitcast.2, bf16[8192,128]{1,0:T(8,128)(2,1)} %proto_ref.1), custom_call_target="tpu_custom_call" | custom-call | tf_op jit(solution)/shard_map/swav_step/pallas_call | solution.py:505
  96.6 0.5 copy.7
  97.1 1.3 %copy.8 = bf16[8192,128]{1,0:T(8,128)(2,1)} copy(bf16[8192,128]{1,0:T(8,128)(2,1)S(1)} %get-tuple-element.9) | data formatting | bytes 4194304
Async XLA Ops:
  0.6 0.8 copy-start
  1.5 0.7 copy-start.1

commit v3 on v2

--- a/solution.py
+++ b/solution.py
@@ -62,8 +62,8 @@
     view_ref, slot_ref, proto_ref, loss_ref, grad_ref,
     view, slot, raw, unit_c, z_own, z_mine, z_other, expo, soft, weighted, z_scaled, grad_soft,
     col_wide, col_part, col_got, col_scale, row_part, row_got, row_scale, row_sum, more_part, more_got,
-    half_send, half_got, half_own, half_out, piece_got, shard, whole, loss_rows, loss_send, loss_got,
-    in_sem, z_send, z_recv, o_send, o_recv, col_ssem, col_rsem, row_ssem, row_rsem,
+    half_send, half_got, half_own, half_out, piece_got, shard, loss_rows, loss_send, loss_got,
+    here_sem, in_sem, z_send, z_recv, o_send, o_recv, col_ssem, col_rsem, row_ssem, row_rsem,
     more_ssem, more_rsem, half_ssem, half_rsem, piece_ssem, piece_rsem, all_ssem, all_rsem,
     near_ssem, near_rsem, pass_ssem, pass_rsem, loss_ssem, loss_rsem, out_sem,
 ):
@@ -75,13 +75,31 @@
     n_row, n_col = X * 4, (Y // 2) * (Z // 2)
     sibling = device(x, y, z, 1 - c)
 
-    def row_peer(step):
-        t = (row_me + step) % n_row
-        return device(t // 4, yh * 2 + (t // 2) % 2, zh * 2 + t % 2, c)
-
-    def col_peer(step):
-        t = (col_me + step) % n_col
-        return t, device(x, (t % (Y // 2)) * 2 + yb, (t // (Y // 2)) * 2 + zb, c)
+    def wrap(value, size):
+        return jnp.where(value >= size, value - size, value)
+
+    z_far = [wrap(z + 2 * k, Z) * (2 * Y) for k in range(Z // 2)]
+    y_far = [wrap(y + 2 * k, Y) * 2 + c for k in range(Y // 2)]
+    z_place = [wrap(zh + k, Z // 2) * (Y // 2) for k in range(Z // 2)]
+    y_place = [wrap(yh + k, Y // 2) for k in range(Y // 2)]
+    x_all = [wrap(x + k, X) for k in range(X)]
+    z_near = [z * (2 * Y), (z + 1 - 2 * zb) * (2 * Y)]
+    y_near = [y * 2 + c, (y + 1 - 2 * yb) * 2 + c]
+
+    col_peers = [
+        (z_place[i] + y_place[j], (z_far[i] + y_far[j], x))
+        for i, j in sorted(
+            ((i, j) for i in range(4) for j in range(4) if i or j),
+            key=lambda p: -min(p[0], 4 - p[0]) - min(p[1], 4 - p[1]),
+        )
+    ]
+    row_peers = [
+        (z_near[i] + y_near[j], x_all[k])
+        for k in (2, 1, 3, 0)
+        for i in range(2)
+        for j in range(2)
+        if i or j or k
+    ]
 
     def block_chip(kind):
         return (yb + kind % 2) % 2, (zb + kind // 2) % 2
@@ -112,13 +130,13 @@
     for fetch in fetches:
         fetch.start()
 
-    def hail_groups(step, unused):
-        hail(col_peer(step)[1])
-        hail(row_peer(step))
-        return unused
-
-    lax.fori_loop(1, 16, hail_groups, 0)
-    for dy, dz in near_steps:
+    along_y = [(z_far[0] + y_far[k], x) for k in (2, 1, 3)]
+    along_z = [(z_far[k] + y_far[0], x) for k in (2, 1, 3)]
+    along_x = [(z_near[0] + y_near[0], x_all[k]) for k in (2, 1, 3)]
+    for target in along_y + along_z + along_x:
+        hail(target)
+    out_y, out_z = 2 * yb - 1, 2 * zb - 1
+    for dy, dz in ((out_y, 0), (0, out_z), (out_y, out_z), (out_y, -out_z), (-out_y, out_z)):
         hail(near(dy, dz))
     for kind in range(1, 4):
         hail(block_peer(kind, 0))
@@ -133,7 +151,7 @@
         chosen = across(slots[v : v + 1])
         pick = (jnp.concatenate([chosen, chosen], axis=1) == lanes).astype(F32).astype(BF16)
         z_own[v] = unit(jnp.dot(pick, view[...], preferred_element_type=F32))
-    pl.semaphore_wait(barrier, 45)
+    pl.semaphore_wait(barrier, 21)
 
     place = quad * 2 + c
     copy_to(z_own.at[1 - c], z_mine.at[place], z_send.at[0], z_recv.at[0], sibling).start()
@@ -143,6 +161,11 @@
                 z_own.at[core], z_mine.at[place], z_send.at[kind], z_recv.at[kind],
                 block_peer(kind, core),
             ).start()
+    for n, peers in enumerate((along_y, along_x)):
+        for target in peers:
+            pl.semaphore_signal(
+                here_sem.at[n], inc=1, device_id=target, device_id_type=MESH
+            )
     z_mine[place] = z_own[c]
     fetches[2].wait()
 
@@ -154,14 +177,11 @@
     lax.fori_loop(0, 8, normalise, 0)
 
     def send_columns(it, h):
-        def send(step, unused):
+        for _, target in col_peers:
             copy_to(
                 col_part.at[it, h], col_got.at[it, h, col_me], col_ssem.at[it, h],
-                col_rsem.at[it, h], col_peer(step)[1],
+                col_rsem.at[it, h], target,
             ).start()
-            return unused
-
-        lax.fori_loop(1, n_col, send, 0)
         col_got[it, h, col_me] = col_part[it, h]
 
     def wait_columns(it, h):
@@ -202,6 +222,9 @@
             return total + terms
 
         total = jnp.zeros((8, 256), F32)
+        if kind == 3:
+            pl.semaphore_wait(here_sem.at[0], 3)
+            pl.semaphore_wait(here_sem.at[1], 3)
         if kind < 3:
             total = lax.fori_loop(0, 8, first, total, unroll=2)
         else:
@@ -220,11 +243,8 @@
     to_other.start()
 
     def send_rows(part, got, ssem, rsem):
-        def send(step, unused):
-            copy_to(part, got.at[row_me], ssem, rsem, row_peer(step)).start()
-            return unused
-
-        lax.fori_loop(1, n_row, send, 0)
+        for target in row_peers:
+            copy_to(part, got.at[row_me], ssem, rsem, target).start()
         got[row_me] = part[...]
 
     def wait_rows(got, rsem):
@@ -349,14 +369,10 @@
         both = half_own[m] + half_got[m].astype(F32)
         half_out[m] = both.astype(BF16).reshape(16, PIECE, L)
 
-        def send(step, unused):
-            t, target = col_peer(step)
+        for t, target in col_peers:
             copy_to(
                 half_out.at[m, t], piece_got.at[m, col_me], piece_ssem.at[m], piece_rsem.at[m], target
             ).start()
-            return unused
-
-        lax.fori_loop(1, n_col, send, 0)
         piece_got[m, col_me] = half_out[m, col_me]
 
     away(0)
@@ -378,7 +394,12 @@
     loss_copy.start()
 
     def at_place(spot, m, start, count):
-        return whole.at[spot, pl.ds(m * ROWS + start, count)]
+        return grad_ref.at[pl.ds(spot * 1024 + m * ROWS + start, count)]
+
+    def own_copy(m):
+        return pltpu.make_async_copy(
+            shard.at[m], at_place(place, m, col_me * PIECE, PIECE), out_sem.at[m]
+        )
 
     for m in range(CHUNKS):
         bytes_of(piece_got.at[m, pl.ds(0, n_col - 1)], piece_rsem.at[m])
@@ -387,15 +408,12 @@
             summed = summed + piece_got[m, n].astype(F32)
         shard[m] = summed.astype(BF16)
 
-        def send_shard(step, unused, m=m):
+        for _, target in col_peers:
             copy_to(
                 shard.at[m], at_place(place, m, col_me * PIECE, PIECE), all_ssem.at[m],
-                all_rsem.at[m], col_peer(step)[1],
+                all_rsem.at[m], target,
             ).start()
-            return unused
-
-        lax.fori_loop(1, n_col, send_shard, 0)
-        whole[place, pl.ds(m * ROWS + col_me * PIECE, PIECE)] = shard[m]
+        own_copy(m).start()
 
     loss_copy.wait()
     mine = pl.ds(place, 1)
@@ -413,14 +431,8 @@
         part = at_place(spot, m, 0, ROWS)
         copy_to(part, part, pass_ssem.at[kind, m], pass_rsem.at[kind, m], sibling).start()
 
-    def write_out(spot, m):
-        pltpu.make_async_copy(
-            at_place(spot, m, 0, ROWS),
-            grad_ref.at[pl.ds(spot * 1024 + m * ROWS, ROWS)],
-            out_sem.at[spot, m],
-        ).start()
-
     for m in range(CHUNKS):
+        own_copy(m).wait()
         bytes_of(at_place(place, m, 0, ROWS - PIECE), all_rsem.at[m])
         for (dy, dz), kind, start in zip(near_steps, kinds, starts):
             part = at_place(place, m, start, fourth if kind == 3 else half)
@@ -428,23 +440,18 @@
                 part, part, near_ssem.at[kind - 1, m], near_rsem.at[kind - 1, m], near(dy, dz)
             ).start()
         hand_over(place, m, 0)
-        write_out(place, m)
     for m in range(CHUNKS):
         for kind in range(1, 4):
             spot = block_quad(kind) * 2 + c
             bytes_of(at_place(spot, m, 0, ROWS), near_rsem.at[kind - 1, m])
             hand_over(spot, m, kind)
-            write_out(spot, m)
     for m in range(CHUNKS):
         for kind in range(4):
             spot = block_quad(kind) * 2 + (1 - c)
             bytes_of(at_place(spot, m, 0, ROWS), pass_rsem.at[kind, m])
-            write_out(spot, m)
 
     for m in range(CHUNKS):
         one = at_place(0, 0, 0, ROWS)
-        for n in range(8):
-            bytes_of(one, out_sem.at[n, m])
         for kind in range(4):
             bytes_of(one, pass_ssem.at[kind, m])
         for kind in range(3):
@@ -490,17 +497,17 @@
         vmem((CHUNKS, 16, PIECE, L), BF16),
         vmem((CHUNKS, 16, PIECE, L), BF16),
         vmem((CHUNKS, PIECE, L), BF16),
-        vmem((8, 1024, L), BF16),
         vmem((3, 8, L), F32),
         vmem((8, L), F32),
         vmem((8, L), F32),
+        pltpu.SemaphoreType.REGULAR((2,)),
         dma((3,)), dma((4,)), dma((4,)), dma, dma,
         dma((ITERS, 2)), dma((ITERS, 2)), dma((ITERS,)), dma((ITERS,)),
         dma((2,)), dma((2,)),
         dma((CHUNKS,)), dma((CHUNKS,)), dma((CHUNKS,)), dma((CHUNKS,)),
         dma((CHUNKS,)), dma((CHUNKS,)),
         dma((3, CHUNKS)), dma((3, CHUNKS)), dma((4, CHUNKS)), dma((4, CHUNKS)),
-        dma, dma, dma((8, CHUNKS)),
+        dma, dma, dma((CHUNKS,)),
     ]
     loss, grad = pl.pallas_call(
         kernel,

time: 98.6 us -> 94.2 us (0.955)
  Pallas kernels: 94.5 us -> 90.1 us
    pallas_call x1, Pallas kernels: 94.5 us -> 90.1 us  [local(): pl.pallas_call(kernel, out_shape=[jax.ShapeDtypeStruct((1, L), F32), jax....]
where the time goes in v3:
time: 94.2 us; the launch traced here: 94.1 us
  Pallas kernels  90.1 us (96%)
  local copies, waits for them, and re-layouts  3.34 us (4%)
    pallas_call x1, Pallas kernels, local(): pl.pallas_call(kernel, out_shape=[jax.ShapeDtypeStruct((1, L), F32), jax....  90.1 us
    unnamed x6, local copies, waits for them, and re-layouts  3.34 us

profile of v3, /device:TPU:1, one launch (start us, length us, event | category | flops | bytes accessed | tf_op | source)
XLA Modules:
  0.0 94.1 jit_solution(8316188397702459290)
XLA Ops:
  0.6 0.0 copy-start
  0.6 0.8 copy-done
  1.5 0.0 copy-start.1
  1.5 0.7 copy-done.1
  2.1 90.1 %swav_step.1 = (f32[1,128]{1,0:T(1,128)S(1)}, bf16[8192,128]{1,0:T(8,128)(2,1)S(1)}) custom-call(bf16[256,128]{1,0:T(8,128)(2,1)S(1)} %copy-done, s32[2,128]{1,0:T(2,128)S(1)} %bitcast.2, bf16[8192,128]{1,0:T(8,128)(2,1)} %proto_ref.1), custom_call_target="tpu_custom_call" | custom-call | tf_op jit(solution)/shard_map/swav_step/pallas_call | solution.py:512
  92.2 0.5 copy.7
  92.7 1.3 %copy.8 = bf16[8192,128]{1,0:T(8,128)(2,1)} copy(bf16[8192,128]{1,0:T(8,128)(2,1)S(1)} %get-tuple-element.9) | data formatting | bytes 4194304
Async XLA Ops:
  0.6 0.8 copy-start
  1.5 0.7 copy-start.1

commit v4 on v3

--- a/solution.py
+++ b/solution.py
@@ -174,7 +174,7 @@
         unit_c[rows] = unit(raw[rows].astype(F32))
         return unused
 
-    lax.fori_loop(0, 8, normalise, 0)
+    lax.fori_loop(0, 8, normalise, 0, unroll=2)
 
     def send_columns(it, h):
         for _, target in col_peers:
@@ -226,11 +226,11 @@
             pl.semaphore_wait(here_sem.at[0], 3)
             pl.semaphore_wait(here_sem.at[1], 3)
         if kind < 3:
-            total = lax.fori_loop(0, 8, first, total, unroll=2)
+            total = lax.fori_loop(0, 8, first, total, unroll=4)
         else:
             for h in range(2):
                 total = lax.fori_loop(
-                    0, 4, lambda b, t, h=h: first_last(b, t, h=h), total, unroll=2
+                    0, 4, lambda b, t, h=h: first_last(b, t, h=h), total, unroll=4
                 )
                 send_columns(0, h)
         terms = jnp.sum(total, axis=0, keepdims=True)
@@ -271,7 +271,7 @@
                     new.append(acc[q] + fold(here))
                 return new
 
-            acc = lax.fori_loop(0, 8, step, acc, unroll=4)
+            acc = lax.fori_loop(0, 8, step, acc, unroll=8)
         for q in range(4):
             sums = jnp.sum(acc[q], axis=0, keepdims=True)
             row_part[it, q * 2 : q * 2 + 1] = sums[:, :L]
@@ -291,7 +291,7 @@
                 col_part[it, h, pl.ds(b, 1)] = down(wide)
                 return unused
 
-            lax.fori_loop(0, 8, step, 0, unroll=4)
+            lax.fori_loop(0, 8, step, 0, unroll=8)
             send_columns(it, h)
 
     row_pass(0, False)
@@ -375,10 +375,9 @@
             ).start()
         piece_got[m, col_me] = half_out[m, col_me]
 
-    away(0)
-    for m in range(CHUNKS):
-        if m + 1 < CHUNKS:
-            away(m + 1)
+    for m in range(CHUNKS):
+        away(m)
+    for m in range(CHUNKS):
         stay(m)
         scatter(m)
 

time: 94.2 us -> 93.3 us (level)
  Pallas kernels: 90.1 us -> 89.1 us
    pallas_call x1, Pallas kernels: 90.1 us -> 89.1 us  [local(): pl.pallas_call(kernel, out_shape=[jax.ShapeDtypeStruct((1, L), F32), jax....]
where the time goes in v4:
time: 93.3 us; the launch traced here: 93.1 us
  Pallas kernels  89.1 us (95%)
  local copies, waits for them, and re-layouts  3.34 us (4%)
    pallas_call x1, Pallas kernels, local(): pl.pallas_call(kernel, out_shape=[jax.ShapeDtypeStruct((1, L), F32), jax....  89.1 us
    unnamed x6, local copies, waits for them, and re-layouts  3.34 us

profile of v4, /device:TPU:1, one launch (start us, length us, event | category | flops | bytes accessed | tf_op | source)
XLA Modules:
  0.0 93.1 jit_solution(15526808813379884020)
XLA Ops:
  0.6 0.0 copy-start
  0.6 0.8 copy-done
  1.5 0.0 copy-start.1
  1.5 0.7 copy-done.1
  2.1 89.1 %swav_step.1 = (f32[1,128]{1,0:T(1,128)S(1)}, bf16[8192,128]{1,0:T(8,128)(2,1)S(1)}) custom-call(bf16[256,128]{1,0:T(8,128)(2,1)S(1)} %copy-done, s32[2,128]{1,0:T(2,128)S(1)} %bitcast.2, bf16[8192,128]{1,0:T(8,128)(2,1)} %proto_ref.1), custom_call_target="tpu_custom_call" | custom-call | tf_op jit(solution)/shard_map/swav_step/pallas_call | solution.py:511
  91.3 0.5 copy.7
  91.8 1.3 %copy.8 = bf16[8192,128]{1,0:T(8,128)(2,1)} copy(bf16[8192,128]{1,0:T(8,128)(2,1)S(1)} %get-tuple-element.9) | data formatting | bytes 4194304
Async XLA Ops:
  0.6 0.8 copy-start
  1.5 0.7 copy-start.1

commit v5 on v4

--- a/solution.py
+++ b/solution.py
@@ -174,7 +174,7 @@
         unit_c[rows] = unit(raw[rows].astype(F32))
         return unused
 
-    lax.fori_loop(0, 8, normalise, 0, unroll=2)
+    lax.fori_loop(0, 8, normalise, 0, unroll=4)
 
     def send_columns(it, h):
         for _, target in col_peers:
@@ -226,7 +226,7 @@
             pl.semaphore_wait(here_sem.at[0], 3)
             pl.semaphore_wait(here_sem.at[1], 3)
         if kind < 3:
-            total = lax.fori_loop(0, 8, first, total, unroll=4)
+            total = lax.fori_loop(0, 8, first, total, unroll=8)
         else:
             for h in range(2):
                 total = lax.fori_loop(

time: 93.3 us -> 92.3 us (0.989)
  Pallas kernels: 89.1 us -> 88.1 us
    pallas_call x1, Pallas kernels: 89.1 us -> 88.1 us  [local(): pl.pallas_call(kernel, out_shape=[jax.ShapeDtypeStruct((1, L), F32), jax....]
where the time goes in v5:
time: 92.3 us; the launch traced here: 92.1 us
  Pallas kernels  88.1 us (95%)
  local copies, waits for them, and re-layouts  3.34 us (4%)
    pallas_call x1, Pallas kernels, local(): pl.pallas_call(kernel, out_shape=[jax.ShapeDtypeStruct((1, L), F32), jax....  88.1 us
    unnamed x6, local copies, waits for them, and re-layouts  3.34 us

profile of v5, /device:TPU:1, one launch (start us, length us, event | category | flops | bytes accessed | tf_op | source)
XLA Modules:
  0.0 92.1 jit_solution(12498126662456390873)
XLA Ops:
  0.6 0.0 copy-start
  0.6 0.8 copy-done
  1.5 0.0 copy-start.1
  1.5 0.7 copy-done.1
  2.1 88.1 %swav_step.1 = (f32[1,128]{1,0:T(1,128)S(1)}, bf16[8192,128]{1,0:T(8,128)(2,1)S(1)}) custom-call(bf16[256,128]{1,0:T(8,128)(2,1)S(1)} %copy-done, s32[2,128]{1,0:T(2,128)S(1)} %bitcast.2, bf16[8192,128]{1,0:T(8,128)(2,1)} %proto_ref.1), custom_call_target="tpu_custom_call" | custom-call | tf_op jit(solution)/shard_map/swav_step/pallas_call | solution.py:511
  90.3 0.5 copy.7
  90.8 1.3 %copy.8 = bf16[8192,128]{1,0:T(8,128)(2,1)} copy(bf16[8192,128]{1,0:T(8,128)(2,1)S(1)} %get-tuple-element.9) | data formatting | bytes 4194304
Async XLA Ops:
  0.6 0.8 copy-start
  1.5 0.7 copy-start.1
